TPU v7x, 32 devices: a whole 2x2x4 slice. The times are simulated.
32 devices in a mesh: dp: 16 (over z, x, core), tensor: 2 (over y).
Axes of the slice: x: 2, y: 2, z: 4, core: 2. Of those that a mesh axis runs over, the one named last changes fastest.
Arguments:
- tokens: bfloat16 [6304, 768], P(('dp', 'tensor')), may hold values from -6 to 6
- w_qkv: bfloat16 [768, 3, 768], P('dp', None, 'tensor'), may hold values from -0.21875 to 0.21875
- w_mix: bfloat16 [768, 768], P('dp', 'tensor'), may hold values from -0.875 to 0.875
- w_router: bfloat16 [768, 16], P('dp'), may hold values from -0.15625 to 0.15625
- gain_one: bfloat16 [768], P('dp'), may hold values from 0.5 to 1.5
- shift_one: bfloat16 [768], P('dp'), may hold values from -1 to 1
- gain_two: bfloat16 [768], P('dp'), may hold values from 0.5 to 1.5
- shift_two: bfloat16 [768], P('dp'), may hold values from -1 to 1
- w_expand: bfloat16 [16, 768, 3072], P('dp', None, 'tensor'), may hold values from -0.21875 to 0.21875
- w_shrink: bfloat16 [16, 3072, 768], P('dp', 'tensor'), may hold values from -0.109375 to 0.109375
- expert_ids: int32 [6304, 2], P('dp'), may hold values from 0 to 15, as said below
- slot_ids: int32 [6304, 2], P('dp'), may hold values from 0 to 63, as said below
- keep_mask: int32 [6304, 2], P('dp'), may hold values from 0 to 1
- out_grad: bfloat16 [6304, 768], P(('dp', 'tensor')), may hold values from -6 to 6
Outputs:
- block_out: bfloat16 [6304, 768], P(('dp', 'tensor'))
- grad_tokens: float32 [6304, 768], P(('dp', 'tensor'))
- grad_w_qkv: float32 [768, 3, 768], P('dp', None, 'tensor')
- grad_w_mix: float32 [768, 768], P('dp', 'tensor')
- grad_router: float32 [768, 16], P(('dp', 'tensor'))
- grad_gain_one: float32 [768], P(('dp', 'tensor'))
- grad_shift_one: float32 [768], P(('dp', 'tensor'))
- grad_gain_two: float32 [768], P(('dp', 'tensor'))
- grad_shift_two: float32 [768], P(('dp', 'tensor'))
- grad_w_expand: float32 [16, 768, 3072], P('dp', None, 'tensor')
- grad_w_shrink: float32 [16, 3072, 768], P('dp', 'tensor')
Inputs may be any that keep to these rules, and one draw needn't show every extreme that they name: `expert_ids`: the two experts of a token differ. `slot_ids`: among the kept routes of the 394 rows of one index of dp, no two share an expert and a slot; a dropped route has slot 0.
All inputs are finite; a program needn't handle non-finite values.
Results may differ from a plain program's by a relative error of at most 0.017.
Values may be sent and summed in bfloat16 or wider, within the bound.
A program may use at most 128 MiB of HBM per device.

v0:
```python
import jax
import jax.numpy as jnp
from jax import lax
from jax.sharding import PartitionSpec as P

DH = 64
SEQ = 197


def norm_rows(values, gain, shift):
    centre = values - jnp.mean(values, axis=-1, keepdims=True)
    spread = jnp.mean(centre * centre, axis=-1, keepdims=True)
    return centre * lax.rsqrt(spread + 1e-06) * gain + shift


def fetch(shards):
    return (
        lax.all_gather(shards[0], "dp", axis=0, tiled=True),
        lax.all_gather(shards[1], "dp", axis=0, tiled=True),
        lax.all_gather(shards[2], "dp", axis=0, tiled=True),
        lax.all_gather(shards[3], "dp", axis=0, tiled=True),
        lax.all_gather(shards[4], "dp", axis=0, tiled=True),
        lax.all_gather(shards[5], "dp", axis=0, tiled=True),
        lax.all_gather(shards[6], "dp", axis=0, tiled=True),
    )


def share_rows(values):
    return lax.all_gather(values, "tensor", axis=0, tiled=True)


def reduce_rows(values):
    return lax.psum_scatter(
        values.astype(jnp.bfloat16), "tensor", scatter_dimension=0, tiled=True
    ).astype(jnp.float32)


def send_out(buffer):
    return lax.all_to_all(buffer, "dp", split_axis=0, concat_axis=0, tiled=True)


def pick_routes(buffer, dest):
    width = buffer.shape[-1]
    flat = jnp.concatenate([buffer.reshape(-1, width), jnp.zeros((1, width), buffer.dtype)], 0)
    return (
        jnp.take(flat, dest.reshape(-1), axis=0)
        .reshape(dest.shape[0], 2, width)
        .astype(jnp.float32)
    )


def bring_back(values, expert_ids, slot_ids, keep_mask):
    experts, slots, width = values.shape
    arrived = lax.all_to_all(values, "dp", split_axis=0, concat_axis=0, tiled=True)
    dest = jnp.where(keep_mask > 0, expert_ids * slots + slot_ids, experts * slots)
    return pick_routes(arrived, dest)


def split_heads(mixed, images, head_size):
    heads = mixed.shape[2] // head_size
    shaped = mixed.reshape(images, -1, 3, heads, head_size)
    return (shaped[:, :, 0], shaped[:, :, 1], shaped[:, :, 2])


def attend(mixed, images, head_size):
    query, key_rows, value_rows = split_heads(mixed, images, head_size)
    scores = jnp.einsum(
        "ishd,ithd->ihst", query, key_rows, preferred_element_type=jnp.float32
    ) * head_size ** (-0.5)
    highest_score = jnp.max(scores, axis=-1, keepdims=True)
    total = jnp.sum(jnp.exp(scores - highest_score), axis=-1, keepdims=True)
    log_total = highest_score + jnp.log(total)
    weights = jnp.exp(scores - log_total).astype(jnp.bfloat16)
    heads_out = jnp.einsum(
        "ihst,ithd->ishd", weights, value_rows, preferred_element_type=jnp.float32
    )
    return (heads_out.reshape(mixed.shape[0], -1).astype(jnp.bfloat16), log_total)


def attend_back(mixed, log_total, grad_heads, images, head_size):
    query, key_rows, value_rows = split_heads(mixed, images, head_size)
    scale = head_size ** (-0.5)
    scores = (
        jnp.einsum("ishd,ithd->ihst", query, key_rows, preferred_element_type=jnp.float32) * scale
    )
    probs = jnp.exp(scores - log_total)
    weights = probs.astype(jnp.bfloat16)
    grad_shaped = grad_heads.reshape(query.shape)
    grad_weights = jnp.einsum(
        "ishd,ithd->ihst", grad_shaped, value_rows, preferred_element_type=jnp.float32
    )
    grad_values = jnp.einsum(
        "ihst,ishd->ithd", weights, grad_shaped, preferred_element_type=jnp.float32
    )
    grad_scores = (
        probs * (grad_weights - jnp.sum(probs * grad_weights, axis=-1, keepdims=True))
    ).astype(jnp.bfloat16)
    grad_query = (
        jnp.einsum("ihst,ithd->ishd", grad_scores, key_rows, preferred_element_type=jnp.float32)
        * scale
    )
    grad_keys = (
        jnp.einsum("ihst,ishd->ithd", grad_scores, query, preferred_element_type=jnp.float32)
        * scale
    )
    stacked = jnp.stack([grad_query, grad_keys, grad_values], axis=2)
    return stacked.reshape(mixed.shape[0], 3, -1)


def body(
    tokens,
    w_qkv,
    w_mix,
    w_router,
    gain_one,
    shift_one,
    gain_two,
    shift_two,
    w_expand,
    w_shrink,
    expert_ids,
    slot_ids,
    keep_mask,
    out_grad,
):
    highest = lax.Precision.HIGHEST
    contract_rows = (((0,), (0,)), ((), ()))
    contract_cols = (((1,), (1,)), ((), ()))
    width = tokens.shape[1]
    group = expert_ids.shape[0]
    images = group // SEQ
    experts = lax.axis_size("dp")
    slots = 2 * max(1, 2 * group * 2 // 3 // experts)
    shards = (w_qkv, w_mix, w_router, gain_one, shift_one, gain_two, shift_two)
    qkv_full, mix_full, router_full, gain_a, shift_a, gain_b, shift_b = fetch(shards)
    gain_a = gain_a.astype(jnp.float32)
    shift_a = shift_a.astype(jnp.float32)
    gain_b = gain_b.astype(jnp.float32)
    shift_b = shift_b.astype(jnp.float32)
    resid = tokens.astype(jnp.float32)
    group_a = share_rows(norm_rows(resid, gain_a, shift_a).astype(jnp.bfloat16))
    mixed = jnp.einsum("rd,dcf->rcf", group_a, qkv_full, preferred_element_type=jnp.float32).astype(
        jnp.bfloat16
    )
    heads_out, log_total = attend(mixed, images, DH)
    branch_a = lax.psum_scatter(
        lax.dot_general(
            heads_out, mix_full, contract_cols, preferred_element_type=jnp.float32
        ).astype(jnp.bfloat16),
        "tensor",
        scatter_dimension=0,
        tiled=True,
    ).astype(jnp.float32)
    resid_b = resid + branch_a
    group_b = share_rows(norm_rows(resid_b, gain_b, shift_b).astype(jnp.bfloat16))
    logits = jnp.dot(group_b, router_full, preferred_element_type=jnp.float32)
    onehot = expert_ids[:, :, None] == jnp.arange(experts, dtype=jnp.int32)[None, None, :]
    chosen = jnp.sum(jnp.where(onehot, logits[:, None, :], 0.0), axis=-1)
    pick = jax.nn.softmax(chosen, axis=-1)
    keep_float = keep_mask.astype(jnp.float32)
    gates = pick * keep_float
    dest = jnp.where(keep_mask > 0, expert_ids * slots + slot_ids, experts * slots)
    route_index = jnp.arange(2 * group, dtype=jnp.int32).reshape(group, 2)
    table = jnp.full((experts * slots + 1,), 2 * group, jnp.int32)
    table = table.at[dest.reshape(-1)].set(route_index.reshape(-1))[:-1]
    padded_rows = jnp.concatenate([group_b, jnp.zeros((1, width), jnp.bfloat16)], 0)
    sent = jnp.take(padded_rows, table // 2, axis=0).reshape(experts, slots, width)
    arrived = send_out(sent).reshape(-1, width)
    expand_here = w_expand[0]
    shrink_here = w_shrink[0]
    inner = jnp.dot(arrived, expand_here, preferred_element_type=jnp.float32)
    active = jax.nn.gelu(inner).astype(jnp.bfloat16)
    result = jnp.dot(active, shrink_here, preferred_element_type=jnp.float32).astype(jnp.bfloat16)
    route_out = bring_back(result.reshape(experts, slots, width), expert_ids, slot_ids, keep_mask)
    branch_b = reduce_rows(jnp.sum(gates[:, :, None] * route_out, axis=1))
    block_out = (resid_b + branch_b).astype(jnp.bfloat16)
    grad_out = out_grad.astype(jnp.float32)
    grad_group = share_rows(out_grad).astype(jnp.float32)
    route_grad = (gates[:, :, None] * grad_group[:, None, :]).astype(jnp.bfloat16)
    grad_gate = jnp.sum(grad_group[:, None, :] * route_out, axis=-1)
    padded_grad = jnp.concatenate(
        [route_grad.reshape(-1, width), jnp.zeros((1, width), jnp.bfloat16)], 0
    )
    grad_sent = jnp.take(padded_grad, table, axis=0).reshape(experts, slots, width)
    grad_result = send_out(grad_sent).reshape(-1, width)
    grad_active = lax.dot_general(
        grad_result, shrink_here, contract_cols, preferred_element_type=jnp.float32
    )
    grad_shrink = lax.dot_general(
        active, grad_result, contract_rows, preferred_element_type=jnp.float32
    )
    gelu_value, gelu_pull = jax.vjp(jax.nn.gelu, inner)
    grad_inner = gelu_pull(grad_active)[0].astype(jnp.bfloat16)
    grad_expand = lax.dot_general(
        arrived, grad_inner, contract_rows, preferred_element_type=jnp.float32
    )
    grad_arrived = lax.dot_general(
        grad_inner, expand_here, contract_cols, preferred_element_type=jnp.float32
    ).astype(jnp.bfloat16)
    grad_routes = bring_back(
        grad_arrived.reshape(experts, slots, width), expert_ids, slot_ids, keep_mask
    )
    grad_pick = keep_float * grad_gate
    grad_chosen = pick * (grad_pick - jnp.sum(pick * grad_pick, axis=-1, keepdims=True))
    grad_logits = jnp.sum(jnp.where(onehot, grad_chosen[:, :, None], 0.0), axis=1)
    router_float = router_full.astype(jnp.float32)
    grad_router = lax.dot_general(
        group_b.astype(jnp.float32), grad_logits, contract_rows, precision=highest
    )
    grad_normed_b = jnp.sum(grad_routes, axis=1) + lax.dot_general(
        grad_logits, router_float, contract_cols, precision=highest
    )
    grad_normed_b = reduce_rows(grad_normed_b)
    norm_value_b, norm_pull_b = jax.vjp(norm_rows, resid_b, gain_b, shift_b)
    grad_resid_b, grad_gain_b, grad_shift_b = norm_pull_b(grad_normed_b)
    grad_resid_b = grad_resid_b + grad_out
    grad_branch = share_rows(grad_resid_b.astype(jnp.bfloat16))
    grad_mix = lax.dot_general(
        grad_branch, heads_out, contract_rows, preferred_element_type=jnp.float32
    )
    grad_heads = jnp.dot(grad_branch, mix_full, preferred_element_type=jnp.float32).astype(
        jnp.bfloat16
    )
    grad_mixed = attend_back(mixed, log_total, grad_heads, images, DH).astype(jnp.bfloat16)
    grad_qkv = jnp.einsum("rd,rcf->dcf", group_a, grad_mixed, preferred_element_type=jnp.float32)
    grad_normed_a = reduce_rows(
        jnp.einsum("rcf,dcf->rd", grad_mixed, qkv_full, preferred_element_type=jnp.float32)
    )
    norm_value_a, norm_pull_a = jax.vjp(norm_rows, resid, gain_a, shift_a)
    grad_resid_a, grad_gain_a, grad_shift_a = norm_pull_a(grad_normed_a)
    grad_tokens = grad_resid_a + grad_resid_b
    summed_weights = (
        lax.psum_scatter(grad_qkv, "dp", scatter_dimension=0, tiled=True),
        lax.psum_scatter(grad_mix, "dp", scatter_dimension=0, tiled=True),
    )
    summed_small = (
        lax.psum_scatter(grad_router, ("dp", "tensor"), scatter_dimension=0, tiled=True),
        lax.psum_scatter(grad_gain_a, ("dp", "tensor"), scatter_dimension=0, tiled=True),
        lax.psum_scatter(grad_shift_a, ("dp", "tensor"), scatter_dimension=0, tiled=True),
        lax.psum_scatter(grad_gain_b, ("dp", "tensor"), scatter_dimension=0, tiled=True),
        lax.psum_scatter(grad_shift_b, ("dp", "tensor"), scatter_dimension=0, tiled=True),
    )
    return (
        block_out,
        grad_tokens,
        summed_weights[0],
        summed_weights[1],
        summed_small[0],
        summed_small[1],
        summed_small[2],
        summed_small[3],
        summed_small[4],
        grad_expand[None],
        grad_shrink[None],
    )


def solution(mesh):
    placed = (
        P(("dp", "tensor"), None),
        P("dp", None, "tensor"),
        P("dp", "tensor"),
        P("dp", None),
        P("dp"),
        P("dp"),
        P("dp"),
        P("dp"),
        P("dp", None, "tensor"),
        P("dp", "tensor", None),
        P("dp", None),
        P("dp", None),
        P("dp", None),
        P(("dp", "tensor"), None),
    )
    return jax.shard_map(
        body,
        mesh=mesh,
        in_specs=placed,
        out_specs=(
            P(("dp", "tensor"), None),
            P(("dp", "tensor"), None),
            P("dp", None, "tensor"),
            P("dp", "tensor"),
            P(("dp", "tensor"), None),
            P(("dp", "tensor")),
            P(("dp", "tensor")),
            P(("dp", "tensor")),
            P(("dp", "tensor")),
            P("dp", None, "tensor"),
            P("dp", "tensor", None),
        ),
        check_vma=False,
    )
```

profile of v0, /device:TPU:0, one launch (start us, length us, event | category | flops | bytes accessed | tf_op | source)
XLA Modules:
  0.0 587.7 jit_solution(10345280353186968672)
XLA Ops:
  13.2 36.4 %all-reduce.22 = (bf16[768]{0:T(1024)(128)(2,1)}, bf16[768]{0:T(1024)(128)(2,1)}, bf16[768]{0:T(1024)(128)(2,1)S(1)}, bf16[768]{0:T(1024)(128)(2,1)S(1)}) all-reduce(bf16[768]{0:T(1024)(128)(2,1)S(1)} %dynamic-update-slice.3, bf16[768]{0:T(1024)(128)(2,1)S(1)} %dynamic-update-slice.2, ...), channel_id=1, replica_groups=mesh['dp'=16,'tensor'=2] {'dp'}, use_global_device_ids=true, to_apply=%add.7 | all-reduce | flops 3072 | bytes 12288
  50.7 5.3 scatter_custom_fusion
  59.6 7.5 %all-gather = bf16[2,197,768]{2,1,0:T(8,128)(2,1)S(1)} all-gather(bf16[1,197,768]{2,1,0:T(8,128)(2,1)S(1)} %fusion.65), channel_id=1, replica_groups=mesh['dp'=16,'tensor'=2] {'tensor'}, dimensions={0}, use_global_device_ids=true | all-gather | bytes 907776 | tf_op jit(solution)/shard_map/all_gather | solution.py:29
  68.1 20.3 %all_gather.37 = bf16[768,384]{1,0:T(8,128)(2,1)} all-gather(bf16[48,384]{1,0:T(8,128)(2,1)S(1)} %copy-done.31), channel_id=1, replica_groups=mesh['dp'=16,'tensor'=2] {'dp'}, dimensions={0}, use_global_device_ids=true | all-gather | bytes 626688 | tf_op jit(solution)/shard_map/all_gather | solution.py:19
  110.9 13.1 %fusion = bf16[200,768]{1,0:T(8,128)(2,1)S(1)} fusion(bf16[394,768]{1,0:T(8,128)(2,1)} %convolution_convert_fusion.1), kind=kCustom, calls=%all-reduce-scatter | all-reduce-scatter fusion | flops 307201 | bytes 912896
  129.2 8.9 %all-gather.1 = bf16[2,197,768]{2,1,0:T(8,128)(2,1)} all-gather(bf16[1,197,768]{2,1,0:T(8,128)(2,1)S(1)} %fusion.64), channel_id=1, replica_groups=mesh['dp'=16,'tensor'=2] {'tensor'}, dimensions={0}, use_global_device_ids=true | all-gather | bytes 907776 | tf_op jit(solution)/shard_map/all_gather | solution.py:29
  141.2 5.2 gather_fusion
  148.2 39.5 %all_to_all.20 = bf16[16,64,768]{2,1,0:T(8,128)(2,1)S(1)} all-to-all(bf16[16,64,768]{2,1,0:T(8,128)(2,1)S(1)} %broadcast_select_fusion.1), channel_id=1, replica_groups=mesh['dp'=16,'tensor'=2] {'dp'}, dimensions={0} | all-to-all | bytes 3145728 | tf_op jit(solution)/shard_map/all_to_all | solution.py:39
  191.5 4.8 fusion.24
  196.4 5.2 all-to-all-start.1
  201.8 42.1 %all-gather.2 = bf16[16,48,16]{1,2,0:T(8,128)(2,1)S(1)} all-gather(bf16[1,48,16]{1,2,0:T(8,128)(2,1)S(1)} %bitcast.127), channel_id=1, replica_groups=mesh['dp'=16,'tensor'=2] {'dp'}, dimensions={0}, use_global_device_ids=true | all-gather | bytes 26112 | tf_op jit(solution)/shard_map/all_gather | solution.py:20
  244.0 10.3 %all-gather.3 = bf16[2,197,768]{2,1,0:T(8,128)(2,1)} all-gather(bf16[1,197,768]{2,1,0:T(8,128)(2,1)S(1)} %bitcast.122), channel_id=1, replica_groups=mesh['dp'=16,'tensor'=2] {'tensor'}, dimensions={0}, use_global_device_ids=true | all-gather | bytes 907776 | tf_op jit(solution)/shard_map/all_gather | solution.py:29
  260.1 4.2 mul.257
  267.4 6.4 %gather_fusion.2 = bf16[788,768]{1,0:T(8,128)(2,1)} fusion(bf16[1025,768]{1,0:T(8,128)(2,1)} %concatenate.15, s32[1024]{0:T(1024)S(1)} %pad_clamp_fusion), kind=kCustom, calls=%fused_computation.clone | custom fusion | bytes 2423888 | tf_op jit(solution)/shard_map/jit(_take)/gather | solution.py:46
  280.0 7.0 %gather_fusion.1 = bf16[1024,768]{1,0:T(8,128)(2,1)} fusion(bf16[789,768]{1,0:T(8,128)(2,1)} %concatenate.16, s32[1024]{0:T(1024)S(1)} %get-tuple-element.44), kind=kCustom, calls=%fused_computation.3 | custom fusion | bytes 3149824 | tf_op jit(solution)/shard_map/jit(_take)/gather | solution.py:184
  288.6 55.6 %all_to_all.21 = bf16[16,64,768]{2,1,0:T(8,128)(2,1)S(1)} all-to-all(bf16[16,64,768]{2,1,0:T(8,128)(2,1)S(1)} %broadcast_select_fusion), channel_id=1, replica_groups=mesh['dp'=16,'tensor'=2] {'dp'}, dimensions={0} | all-to-all | bytes 3145728 | tf_op jit(solution)/shard_map/all_to_all | solution.py:39
  344.2 8.3 %fusion.10 = bf16[1024,1536]{1,0:T(8,128)(2,1)S(1)} fusion(f32[1024,1536]{1,0:T(8,128)} %copy-done.49, bf16[1024,768]{1,0:T(8,128)(2,1)S(1)} %bitcast.123, bf16[1,1536,768]{2,1,0:T(8,128)(2,1)S(1)} %copy-done), kind=kOutput, calls=%fused_computation.13 | convolution fusion | flops 2447376384 | bytes 13369344 | tf_op jit(solution)/shard_map/dot_general | solution.py:186
  356.2 5.0 all-to-all-start.3
  361.3 31.9 %all-to-all-done.3 = bf16[16,64,768]{2,1,0:T(8,128)(2,1)S(1)} async-done(((bf16[16,64,768]{2,1,0:T(8,128)(2,1)}), bf16[16,64,768]{2,1,0:T(8,128)(2,1)S(1)}, u32[]{:S(2)}, u32[]{:S(2)}) %all-to-all-start.3) | async-done | bytes 1572896 | tf_op jit(solution)/shard_map/all_to_all | solution.py:54
  395.9 4.1 gather_fusion.3
  400.0 4.3 select_convert_fusion
  404.2 4.0 reshape.229
  408.3 4.6 reduce_sum.202
  413.5 12.9 %fusion.2 = bf16[200,768]{1,0:T(8,128)(2,1)S(1)} fusion(bf16[394,768]{1,0:T(8,128)(2,1)S(1)} %fusion.29), kind=kCustom, calls=%all-reduce-scatter.2 | all-reduce-scatter fusion | flops 307201 | bytes 912896
  432.7 9.1 %all-gather.4 = bf16[2,197,768]{2,1,0:T(8,128)(2,1)S(1)} all-gather(bf16[1,197,768]{2,1,0:T(8,128)(2,1)S(1)} %fusion.63), channel_id=1, replica_groups=mesh['dp'=16,'tensor'=2] {'tensor'}, dimensions={0}, use_global_device_ids=true | all-gather | bytes 907776 | tf_op jit(solution)/shard_map/all_gather | solution.py:29
  471.9 8.7 %convolution_bitcast_fusion = f32[1,1536,768]{2,1,0:T(8,128)} fusion(bf16[1024,768]{1,0:T(8,128)(2,1)S(1)} %bitcast.124, f32[1024,1536]{1,0:T(8,128)} %copy-done.49), kind=kOutput, calls=%fused_computation.15 | convolution fusion | flops 2430074880 | bytes 12582912 | tf_op jit(solution)/shard_map/dot_general | solution.py:189
  480.6 4.0 reshape.228
  484.6 4.9 multiply_reduce_fusion.2
  491.3 17.0 %fusion.83 = (bf16[200,768]{1,0:T(8,128)(2,1)S(1)}, bf16[200,768]{1,0:T(8,128)(2,1)}) fusion(bf16[394,768]{1,0:T(8,128)(2,1)S(1)} %multiply_reduce_fusion.2, bf16[394,768]{1,0:T(8,128)(2,1)} %fusion.28), kind=kCustom, calls=%all-reduce-scatter.4 | all-reduce-scatter fusion | flops 614401 | bytes 1825280
  512.5 6.4 %convolution_bitcast_fusion.1 = f32[1,768,1536]{2,1,0:T(8,128)} fusion(bf16[1024,768]{1,0:T(8,128)(2,1)S(1)} %bitcast.118, bf16[1024,1536]{1,0:T(8,128)(2,1)} %copy-done.20), kind=kOutput, calls=%fused_computation.16 | convolution fusion | flops 2415919104 | bytes 9437184 | tf_op jit(solution)/shard_map/dot_general | solution.py:194
  523.3 44.1 %all-reduce.21 = (f32[768,16]{0,1:T(8,128)S(1)}, f32[768]{0:T(1024)S(1)}, f32[768]{0:T(1024)S(1)}, f32[768]{0:T(1024)S(1)}, f32[768]{0:T(1024)S(1)}) all-reduce(f32[768,16]{0,1:T(8,128)S(1)} %fusion.90, f32[768]{0:T(1024)S(1)} %get-tuple-element.14, ...), channel_id=8, replica_groups=mesh['dp'=16,'tensor'=2] {'dp','tensor'}, use_global_device_ids=true, to_apply=%region_26.28.clone | all-reduce | flops 15360 | bytes 122880
  576.3 4.4 reduce-scatter.12.cloned.1.call-done
  (239 shorter events, 125.8 us)
Async XLA Ops:
  7.2 184.4 %copy-start = (bf16[1,1536,768]{2,1,0:T(8,128)(2,1)S(1)}, bf16[1,1536,768]{2,1,0:T(8,128)(2,1)}, u32[]{:S(2)}) copy-start(bf16[1,1536,768]{2,1,0:T(8,128)(2,1)} %param.25) | copy-start | bytes 7077892
  7.2 60.9 %copy-start.31 = (bf16[48,384]{1,0:T(8,128)(2,1)S(1)}, bf16[48,384]{1,0:T(8,128)(2,1)}, u32[]{:S(2)}) copy-start(bf16[48,384]{1,0:T(8,128)(2,1)} %param.18) | copy-start | bytes 110596
  7.2 81.2 %all-gather.7.cloned.1.call-start = ((), (), s32[]{:S(2)}) async-start(), calls=%async_computation.6 | async-start | bytes 1880064 | tf_op jit(solution)/shard_map/all_gather | solution.py:18
  50.5 41.5 %copy-start.24 = (s32[394,2]{1,0:T(8,128)}, s32[394,2]{1,0:T(8,128)S(1)}, u32[]{:S(2)}) copy-start(s32[394,2]{1,0:T(8,128)S(1)} %copy.94) | copy-start | bytes 9460
  58.4 33.6 %copy-start.38 = (f32[197]{0:T(256)}, f32[197]{0:T(256)S(1)}, u32[]{:S(2)}) copy-start(f32[197]{0:T(256)S(1)} %fusion.47) | copy-start | bytes 2368
  58.4 33.6 %copy-start.34 = (f32[197]{0:T(256)}, f32[197]{0:T(256)S(1)}, u32[]{:S(2)}) copy-start(f32[197]{0:T(256)S(1)} %fusion.79) | copy-start | bytes 2368
  107.6 18.9 %copy-start.45 = (u32[32]{0:T(128)S(1)}, u32[32]{0:T(128)}, u32[]{:S(2)}) copy-start(u32[32]{0:T(128)} %constant.139) | copy-start | bytes 388
  107.7 20.2 %copy-start.44 = (bf16[768]{0:T(1024)(128)(2,1)S(1)}, bf16[768]{0:T(1024)(128)(2,1)}, u32[]{:S(2)}) copy-start(bf16[768]{0:T(1024)(128)(2,1)} %get-tuple-element.23) | copy-start | bytes 4612
  107.7 20.2 %copy-start.43 = (bf16[768]{0:T(1024)(128)(2,1)S(1)}, bf16[768]{0:T(1024)(128)(2,1)}, u32[]{:S(2)}) copy-start(bf16[768]{0:T(1024)(128)(2,1)} %get-tuple-element.24) | copy-start | bytes 4612
  107.7 20.8 %copy-start.4 = (bf16[197,768]{1,0:T(8,128)(2,1)S(1)}, bf16[197,768]{1,0:T(8,128)(2,1)}, u32[]{:S(2)}) copy-start(bf16[197,768]{1,0:T(8,128)(2,1)} %param.16) | copy-start | bytes 907780
  108.3 19.6 %copy-start.18 = (bf16[394,384]{0,1:T(8,128)(2,1)}, bf16[394,384]{0,1:T(8,128)(2,1)S(1)}, u32[]{:S(2)}) copy-start(bf16[394,384]{0,1:T(8,128)(2,1)S(1)} %convert_element_type.124) | copy-start | bytes 907780
  124.1 3.8 collective-permute-start
  146.5 42.5 %copy-start.46 = (bf16[1,768,1536]{2,1,0:T(8,128)(2,1)S(1)}, bf16[1,768,1536]{2,1,0:T(8,128)(2,1)}, u32[]{:S(2)}) copy-start(bf16[1,768,1536]{2,1,0:T(8,128)(2,1)} %param.24) | copy-start | bytes 7077892
  196.4 47.6 %copy-start.21 = (bf16[197,768]{1,0:T(8,128)(2,1)S(1)}, bf16[197,768]{1,0:T(8,128)(2,1)}, u32[]{:S(2)}) copy-start(bf16[197,768]{1,0:T(8,128)(2,1)} %param.29) | copy-start | bytes 907780
  196.4 68.3 %all-to-all-start.1 = ((bf16[16,64,768]{2,1,0:T(8,128)(2,1)}), bf16[16,64,768]{2,1,0:T(8,128)(2,1)}, u32[]{:S(2)}, u32[]{:S(2)}) async-start(bf16[16,64,768]{2,1,0:T(8,128)(2,1)} %bitcast.125), calls=%async_computation.1 | async-start | bytes 3145728 | tf_op jit(solution)/shard_map/all_to_all | solution.py:54
  356.2 37.0 %all-to-all-start.3 = ((bf16[16,64,768]{2,1,0:T(8,128)(2,1)}), bf16[16,64,768]{2,1,0:T(8,128)(2,1)S(1)}, u32[]{:S(2)}, u32[]{:S(2)}) async-start(bf16[16,64,768]{2,1,0:T(8,128)(2,1)} %bitcast.126), calls=%async_computation.3 | async-start | bytes 3145728 | tf_op jit(solution)/shard_map/all_to_all | solution.py:54
  361.3 215.1 %reduce-scatter.14.cloned.1.call-start = ((), (), s32[]{:S(2)}) async-start(), calls=%async_computation.8 | async-start | bytes 1253376 | tf_op jit(solution)/shard_map/reduce_scatter | solution.py:234
  412.8 18.0 %copy-start.6 = (bf16[203,768]{1,0:T(8,128)(2,1)S(1)}, bf16[203,768]{1,0:T(8,128)(2,1)}, u32[]{:S(2)}) copy-start(bf16[203,768]{1,0:T(8,128)(2,1)} %copy-done.5) | copy-start | bytes 935428
  413.5 19.0 %copy-start.22 = (bf16[197,768]{1,0:T(8,128)(2,1)S(1)}, bf16[197,768]{1,0:T(8,128)(2,1)}, u32[]{:S(2)}) copy-start(bf16[197,768]{1,0:T(8,128)(2,1)} %param.29) | copy-start | bytes 907780
  426.5 3.9 collective-permute-start.2
  432.5 14.7 %copy-start.12 = (f32[197,768]{1,0:T(8,128)}, f32[197,768]{1,0:T(8,128)S(1)}, u32[]{:S(2)}) copy-start(f32[197,768]{1,0:T(8,128)S(1)} %get-tuple-element.32) | copy-start | bytes 1815556
  432.5 14.7 %copy-start.40 = (f32[197]{0:T(256)}, f32[197]{0:T(256)S(1)}, u32[]{:S(2)}) copy-start(f32[197]{0:T(256)S(1)} %negate_multiply_fusion.1) | copy-start | bytes 2368
  447.2 133.5 %reduce-scatter.12.cloned.1.call-start = ((), (), s32[]{:S(2)}) async-start(), calls=%async_computation.7 | async-start | bytes 3760128 | tf_op jit(solution)/shard_map/reduce_scatter | solution.py:233
  489.5 23.0 %copy-start.10 = (bf16[16,64,768]{2,1,0:T(8,128)(2,1)S(1)}, bf16[16,64,768]{2,1,0:T(8,128)(2,1)}, u32[]{:S(2)}) copy-start(bf16[16,64,768]{2,1,0:T(8,128)(2,1)} %copy-done.9) | copy-start | bytes 4718596
  509.0 13.8 %copy-start.39 = (f32[197]{0:T(256)S(1)}, f32[197]{0:T(256)}, u32[]{:S(2)}) copy-start(f32[197]{0:T(256)} %copy-done.38) | copy-start | bytes 2368
  509.0 13.8 %copy-start.35 = (f32[197]{0:T(256)S(1)}, f32[197]{0:T(256)}, u32[]{:S(2)}) copy-start(f32[197]{0:T(256)} %copy-done.34) | copy-start | bytes 2368
  509.0 14.2 %copy-start.36 = (f32[768]{0:T(1024)S(1)}, f32[768]{0:T(1024)}, u32[]{:S(2)}) copy-start(f32[768]{0:T(1024)} %get-tuple-element.12) | copy-start | bytes 9220
  509.0 14.2 %copy-start.37 = (f32[768]{0:T(1024)S(1)}, f32[768]{0:T(1024)}, u32[]{:S(2)}) copy-start(f32[768]{0:T(1024)} %get-tuple-element.16) | copy-start | bytes 9220
  509.1 11.1 %collective-permute-start.3 = (bf16[3,768]{1,0:T(4,128)(2,1)S(1)}, bf16[3,768]{1,0:T(4,128)(2,1)S(1)}, u32[]{:S(2)}, u32[]{:S(2)}) collective-permute-start(bf16[3,768]{1,0:T(4,128)(2,1)S(1)} %slice.37), channel_id=1, source_target_pairs={{0,1},{2,3},{4,5},{6,7},{8,9},{10,11},{12,13},{14,15},{16,17},{18,... | collective-permute-start | bytes 13832
  518.9 54.8 %copy-start.41 = (f32[197]{0:T(256)S(1)}, f32[197]{0:T(256)}, u32[]{:S(2)}) copy-start(f32[197]{0:T(256)} %copy-done.40) | copy-start | bytes 2368
  518.9 50.8 %collective-permute-start.1 = (bf16[3,768]{1,0:T(4,128)(2,1)S(1)}, bf16[3,768]{1,0:T(4,128)(2,1)S(1)}, u32[]{:S(2)}, u32[]{:S(2)}) collective-permute-start(bf16[3,768]{1,0:T(4,128)(2,1)S(1)} %slice.35), channel_id=1, source_target_pairs={{0,1},{2,3},{4,5},{6,7},{8,9},{10,11},{12,13},{14,15},{16,17},{18,... | collective-permute-start | bytes 13832
  520.2 60.5 %copy-start.1 = (bf16[1,1536,768]{2,1,0:T(8,128)(2,1)S(1)}, bf16[1,1536,768]{2,1,0:T(8,128)(2,1)}, u32[]{:S(2)}) copy-start(bf16[1,1536,768]{2,1,0:T(8,128)(2,1)} %param.25) | copy-start | bytes 7077892
  (27 other events, 129.6 us)
Sparse Core Ops, SparseCore 0:
  10.4 43.3 all-gather.6
  447.4 61.6 reduce-scatter.13
  513.5 67.1 reduce-scatter.11
where the time goes:
time: 598 us; the launch traced here: 588 us
  blocking collectives  317 us (53%)
  local copies, waits for them, and re-layouts  101 us (17%)
  matrix products  59.6 us (10%)
  waiting for transfers between devices  38.4 us (6%)
  other arithmetic  35.4 us (6%)
  starting transfers between devices  20.1 us (3%)
  between operations  16.5 us (3%)
    unnamed x5, blocking collectives  123 us
    all_to_all x2, blocking collectives, send_out(): return lax.all_to_all(buffer, 'dp', split_axis=0, concat_axis=0, tiled=True)  95.1 us
    all_gather x1, blocking collectives, fetch(): lax.all_gather(shards[2], 'dp', axis=0, tiled=True)  42.1 us
    all_gather x4, blocking collectives, share_rows(): return lax.all_gather(values, 'tensor', axis=0, tiled=True)  35.8 us
    all_to_all x2, waiting for transfers between devices, bring_back(): lax.all_to_all(values, 'dp', split_axis=0, concat_axis=0, tiled=True)  31.9 us
    unnamed x132, local copies, waits for them, and re-layouts  31.1 us
    all_gather x1, blocking collectives, fetch(): lax.all_gather(shards[1], 'dp', axis=0, tiled=True)  20.3 us
  transfers between devices with their start and end apart: 9, of which 3 were waited for; matrix products, arithmetic and copies ran while one was open for 18% of the time, Pallas kernels for 0%

commit v1 on v0

--- a/solution.py
+++ b/solution.py
@@ -7,6 +7,28 @@
 SEQ = 197
 
 
+def joined_along(blocks, dim):
+    shape = list(blocks.shape[1:])
+    shape[dim] *= blocks.shape[0]
+    return jnp.moveaxis(blocks, 0, dim).reshape(shape)
+
+
+def ring_gather(shard, axis, dim):
+    length = lax.axis_size(axis)
+    pairs = [(i, (i + 1) % length) for i in range(length)]
+    back = [(b, a) for a, b in pairs]
+    lower, upper = ([], [])
+    for step in range(length - 1):
+        if step % 2 == 0:
+            lower.append(lax.ppermute(lower[-1] if lower else shard, axis, pairs))
+        else:
+            upper.append(lax.ppermute(upper[-1] if upper else shard, axis, back))
+    parts = jnp.stack([*lower[::-1], shard, *upper])
+    shift = lax.axis_index(axis) - len(lower)
+    parts = parts[(jnp.arange(length) - shift) % length]
+    return joined_along(parts, dim)
+
+
 def norm_rows(values, gain, shift):
     centre = values - jnp.mean(values, axis=-1, keepdims=True)
     spread = jnp.mean(centre * centre, axis=-1, keepdims=True)
@@ -17,7 +39,7 @@
     return (
         lax.all_gather(shards[0], "dp", axis=0, tiled=True),
         lax.all_gather(shards[1], "dp", axis=0, tiled=True),
-        lax.all_gather(shards[2], "dp", axis=0, tiled=True),
+        ring_gather(shards[2], "dp", 0),
         lax.all_gather(shards[3], "dp", axis=0, tiled=True),
         lax.all_gather(shards[4], "dp", axis=0, tiled=True),
         lax.all_gather(shards[5], "dp", axis=0, tiled=True),

time: 598 us -> 619 us (1.035)
  blocking collectives: 317 us -> 233 us
  waiting for transfers between devices: 38.4 us -> 106 us
  starting transfers between devices: 20.1 us -> 54.7 us
    all_gather x1 -> x0, blocking collectives: 42.1 us -> none  [fetch(): lax.all_gather(shards[2], 'dp', axis=0, tiled=True)]
    all_to_all x2 -> x1, blocking collectives: 95.1 us -> 56.2 us  [send_out(): return lax.all_to_all(buffer, 'dp', split_axis=0, concat_axis=0, tiled=True)]
    ppermute x0 -> x15, waiting for transfers between devices: none -> 36.8 us  [the longest x8 34.2 us: ring_gather(): lower.append(lax.ppermute(lower[-1] if lower else shard, axis, pairs))]
    all_to_all x2, waiting for transfers between devices: 31.9 us -> 62.6 us  [bring_back(): lax.all_to_all(values, 'dp', split_axis=0, concat_axis=0, tiled=True)]
    ppermute x0 -> x15, starting transfers between devices: none -> 30.4 us  [the longest x7 30.1 us: ring_gather(): upper.append(lax.ppermute(upper[-1] if upper else shard, axis, back))]
    unnamed x132 -> x134, local copies, waits for them, and re-layouts: 31.1 us -> 29.1 us
  transfers between devices with their start and end apart: 9 -> 25, of which waited for: 3 -> 10; matrix products, arithmetic and copies ran while one was open for 18% -> 19% of each run, Pallas kernels for 0% -> 0%
where the time goes in v1:
time: 619 us; the launch traced here: 609 us
  blocking collectives  233 us (38%)
  waiting for transfers between devices  106 us (17%)
  local copies, waits for them, and re-layouts  99.5 us (16%)
  matrix products  62.9 us (10%)
  starting transfers between devices  54.7 us (9%)
  other arithmetic  36.5 us (6%)
  between operations  16.6 us (3%)
    unnamed x5, blocking collectives  123 us
    all_to_all x2, waiting for transfers between devices, bring_back(): lax.all_to_all(values, 'dp', split_axis=0, concat_axis=0, tiled=True)  62.6 us
    all_to_all x1, blocking collectives, send_out(): return lax.all_to_all(buffer, 'dp', split_axis=0, concat_axis=0, tiled=True)  56.2 us
    ppermute x8, waiting for transfers between devices, ring_gather(): lower.append(lax.ppermute(lower[-1] if lower else shard, axis, pairs))  34.2 us
    all_gather x4, blocking collectives, share_rows(): return lax.all_gather(values, 'tensor', axis=0, tiled=True)  33.1 us
    ppermute x7, starting transfers between devices, ring_gather(): upper.append(lax.ppermute(upper[-1] if upper else shard, axis, back))  30.1 us
    unnamed x134, local copies, waits for them, and re-layouts  29.1 us
    all_gather x1, blocking collectives, fetch(): lax.all_gather(shards[1], 'dp', axis=0, tiled=True)  20.3 us
  transfers between devices with their start and end apart: 25, of which 10 were waited for; matrix products, arithmetic and copies ran while one was open for 19% of the time, Pallas kernels for 0%

profile of v1, /device:TPU:0, one launch (start us, length us, event | category | flops | bytes accessed | tf_op | source)
XLA Modules:
  0.0 608.6 jit_solution(13231222664455072434)
XLA Ops:
  13.2 36.4 %all-reduce.22 = (bf16[768]{0:T(1024)(128)(2,1)}, bf16[768]{0:T(1024)(128)(2,1)S(1)}, bf16[768]{0:T(1024)(128)(2,1)S(1)}, bf16[768]{0:T(1024)(128)(2,1)S(1)}) all-reduce(bf16[768]{0:T(1024)(128)(2,1)S(1)} %dynamic-update-slice.3, bf16[768]{0:T(1024)(128)(2,1)S(1)} %dynamic-update-slice.2, ...), channel_id=1, replica_groups=mesh['dp'=16,'tensor'=2] {'dp'}, use_global_device_ids=true, to_apply=%add.7 | all-reduce | flops 3072 | bytes 12288
  50.7 5.3 scatter_custom_fusion
  59.6 7.5 %all-gather = bf16[2,197,768]{2,1,0:T(8,128)(2,1)S(1)} all-gather(bf16[1,197,768]{2,1,0:T(8,128)(2,1)S(1)} %fusion.65), channel_id=1, replica_groups=mesh['dp'=16,'tensor'=2] {'tensor'}, dimensions={0}, use_global_device_ids=true | all-gather | bytes 907776 | tf_op jit(solution)/shard_map/all_gather | solution.py:51
  68.1 20.3 %all_gather.34 = bf16[768,384]{1,0:T(8,128)(2,1)} all-gather(bf16[48,384]{1,0:T(8,128)(2,1)S(1)} %copy-done.27), channel_id=1, replica_groups=mesh['dp'=16,'tensor'=2] {'dp'}, dimensions={0}, use_global_device_ids=true | all-gather | bytes 626688 | tf_op jit(solution)/shard_map/all_gather | solution.py:41
  110.9 13.2 %fusion = bf16[200,768]{1,0:T(8,128)(2,1)S(1)} fusion(bf16[394,768]{1,0:T(8,128)(2,1)} %convolution_convert_fusion.1), kind=kCustom, calls=%all-reduce-scatter | all-reduce-scatter fusion | flops 307201 | bytes 912896
  129.2 8.9 %all-gather.1 = bf16[2,197,768]{2,1,0:T(8,128)(2,1)} all-gather(bf16[1,197,768]{2,1,0:T(8,128)(2,1)S(1)} %fusion.64), channel_id=1, replica_groups=mesh['dp'=16,'tensor'=2] {'tensor'}, dimensions={0}, use_global_device_ids=true | all-gather | bytes 907776 | tf_op jit(solution)/shard_map/all_gather | solution.py:51
  141.2 5.2 gather_fusion.1
  149.3 4.5 all-to-all-start
  154.1 30.7 %collective-permute-done = bf16[48,16]{0,1:T(8,128)(2,1)S(1)} collective-permute-done((bf16[48,16]{0,1:T(8,128)(2,1)S(1)}, bf16[48,16]{0,1:T(8,128)(2,1)S(1)}, u32[]{:S(2)}, u32[]{:S(2)}) %collective-permute-start) | collective-permute-done | bytes 1568 | tf_op jit(solution)/shard_map/ppermute | solution.py:23
  184.8 4.4 collective-permute-start.8
  190.6 4.4 collective-permute-start.9
  196.4 4.7 collective-permute-start.10
  202.1 7.6 %all-gather.2 = bf16[2,197,768]{2,1,0:T(8,128)(2,1)} all-gather(bf16[1,197,768]{2,1,0:T(8,128)(2,1)S(1)} %bitcast.153), channel_id=1, replica_groups=mesh['dp'=16,'tensor'=2] {'tensor'}, dimensions={0}, use_global_device_ids=true | all-gather | bytes 907776 | tf_op jit(solution)/shard_map/all_gather | solution.py:51
  234.4 4.4 collective-permute-start.14
  238.9 4.7 fusion.19
  243.6 4.8 fusion.24
  248.4 4.5 all-to-all-start.1
  254.2 30.7 %all-to-all-done.1 = bf16[16,64,768]{2,1,0:T(8,128)(2,1)} async-done(((bf16[16,64,768]{2,1,0:T(8,128)(2,1)}), bf16[16,64,768]{2,1,0:T(8,128)(2,1)}, u32[]{:S(2)}, u32[]{:S(2)}) %all-to-all-start.1) | async-done | bytes 1572896 | tf_op jit(solution)/shard_map/all_to_all | solution.py:76
  287.6 6.4 %gather_fusion.3 = bf16[788,768]{1,0:T(8,128)(2,1)} fusion(bf16[1025,768]{1,0:T(8,128)(2,1)} %concatenate.15, s32[1024]{0:T(1024)S(1)} %pad_clamp_fusion), kind=kCustom, calls=%fused_computation.clone | custom fusion | bytes 2423888 | tf_op jit(solution)/shard_map/jit(_take)/gather | solution.py:68
  300.2 7.0 %gather_fusion.2 = bf16[1024,768]{1,0:T(8,128)(2,1)} fusion(bf16[789,768]{1,0:T(8,128)(2,1)} %concatenate.16, s32[1024]{0:T(1024)S(1)} %get-tuple-element.44), kind=kCustom, calls=%fused_computation.4 | custom fusion | bytes 3149824 | tf_op jit(solution)/shard_map/jit(_take)/gather | solution.py:206
  308.9 56.2 %all_to_all.20 = bf16[16,64,768]{2,1,0:T(8,128)(2,1)S(1)} all-to-all(bf16[16,64,768]{2,1,0:T(8,128)(2,1)S(1)} %broadcast_select_fusion), channel_id=1, replica_groups=mesh['dp'=16,'tensor'=2] {'dp'}, dimensions={0} | all-to-all | bytes 3145728 | tf_op jit(solution)/shard_map/all_to_all | solution.py:61
  365.1 8.3 %fusion.10 = bf16[1024,1536]{1,0:T(8,128)(2,1)S(1)} fusion(f32[1024,1536]{1,0:T(8,128)} %copy-done.43, bf16[1024,768]{1,0:T(8,128)(2,1)S(1)} %bitcast.154, bf16[1,1536,768]{2,1,0:T(8,128)(2,1)S(1)} %copy-done), kind=kOutput, calls=%fused_computation.14 | convolution fusion | flops 2447376384 | bytes 13369344 | tf_op jit(solution)/shard_map/dot_general | solution.py:208
  377.1 5.0 all-to-all-start.3
  382.2 31.9 %all-to-all-done.3 = bf16[16,64,768]{2,1,0:T(8,128)(2,1)S(1)} async-done(((bf16[16,64,768]{2,1,0:T(8,128)(2,1)}), bf16[16,64,768]{2,1,0:T(8,128)(2,1)S(1)}, u32[]{:S(2)}, u32[]{:S(2)}) %all-to-all-start.3) | async-done | bytes 1572896 | tf_op jit(solution)/shard_map/all_to_all | solution.py:76
  429.1 4.6 reduce_sum.202
  434.4 12.9 %fusion.2 = bf16[200,768]{1,0:T(8,128)(2,1)S(1)} fusion(bf16[394,768]{1,0:T(8,128)(2,1)S(1)} %fusion.29), kind=kCustom, calls=%all-reduce-scatter.2 | all-reduce-scatter fusion | flops 307201 | bytes 912896
  453.5 9.1 %all-gather.3 = bf16[2,197,768]{2,1,0:T(8,128)(2,1)S(1)} all-gather(bf16[1,197,768]{2,1,0:T(8,128)(2,1)S(1)} %fusion.63), channel_id=1, replica_groups=mesh['dp'=16,'tensor'=2] {'tensor'}, dimensions={0}, use_global_device_ids=true | all-gather | bytes 907776 | tf_op jit(solution)/shard_map/all_gather | solution.py:51
  492.5 9.1 %convolution_bitcast_fusion = f32[1,1536,768]{2,1,0:T(8,128)} fusion(bf16[1024,768]{1,0:T(8,128)(2,1)} %bitcast.155, f32[1024,1536]{1,0:T(8,128)} %copy-done.43), kind=kOutput, calls=%fused_computation.16 | convolution fusion | flops 2430074880 | bytes 12582912 | tf_op jit(solution)/shard_map/dot_general | solution.py:211
  505.6 4.8 multiply_reduce_fusion.2
  512.3 16.3 %fusion.85 = (bf16[200,768]{1,0:T(8,128)(2,1)S(1)}, bf16[200,768]{1,0:T(8,128)(2,1)S(1)}) fusion(bf16[394,768]{1,0:T(8,128)(2,1)S(1)} %multiply_reduce_fusion.2, bf16[394,768]{1,0:T(8,128)(2,1)} %fusion.28), kind=kCustom, calls=%all-reduce-scatter.4 | all-reduce-scatter fusion | flops 614401 | bytes 1825280
  532.5 7.2 %convolution_bitcast_fusion.1 = f32[1,768,1536]{2,1,0:T(8,128)} fusion(bf16[1024,768]{1,0:T(8,128)(2,1)} %bitcast.25, bf16[1024,1536]{1,0:T(8,128)(2,1)} %copy-done.18), kind=kOutput, calls=%fused_computation.17 | convolution fusion | flops 2415919104 | bytes 9437184 | tf_op jit(solution)/shard_map/dot_general | solution.py:216
  544.1 44.1 %all-reduce.21 = (f32[768,16]{0,1:T(8,128)S(1)}, f32[768]{0:T(1024)S(1)}, f32[768]{0:T(1024)S(1)}, f32[768]{0:T(1024)S(1)}, f32[768]{0:T(1024)S(1)}) all-reduce(f32[768,16]{0,1:T(8,128)S(1)} %fusion.92, f32[768]{0:T(1024)S(1)} %get-tuple-element.14, ...), channel_id=8, replica_groups=mesh['dp'=16,'tensor'=2] {'dp','tensor'}, use_global_device_ids=true, to_apply=%region_26.28.clone | all-reduce | flops 15360 | bytes 122880
  (276 shorter events, 166.7 us)
Async XLA Ops:
  7.2 236.4 %copy-start = (bf16[1,1536,768]{2,1,0:T(8,128)(2,1)S(1)}, bf16[1,1536,768]{2,1,0:T(8,128)(2,1)}, u32[]{:S(2)}) copy-start(bf16[1,1536,768]{2,1,0:T(8,128)(2,1)} %param.25) | copy-start | bytes 7077892
  7.2 60.9 %copy-start.27 = (bf16[48,384]{1,0:T(8,128)(2,1)S(1)}, bf16[48,384]{1,0:T(8,128)(2,1)}, u32[]{:S(2)}) copy-start(bf16[48,384]{1,0:T(8,128)(2,1)} %param.18) | copy-start | bytes 110596
  7.2 81.2 %all-gather.6.cloned.1.call-start = ((), (), s32[]{:S(2)}) async-start(), calls=%async_computation.6 | async-start | bytes 1880064 | tf_op jit(solution)/shard_map/all_gather | solution.py:40
  50.5 41.5 %copy-start.22 = (s32[394,2]{1,0:T(8,128)}, s32[394,2]{1,0:T(8,128)S(1)}, u32[]{:S(2)}) copy-start(s32[394,2]{1,0:T(8,128)S(1)} %copy.94) | copy-start | bytes 9460
  124.1 3.8 collective-permute-start.15
  146.4 42.8 %copy-start.23 = (s32[394,2]{1,0:T(8,128)S(1)}, s32[394,2]{1,0:T(8,128)}, u32[]{:S(2)}) copy-start(s32[394,2]{1,0:T(8,128)} %copy-done.22) | copy-start | bytes 9460
  149.3 52.8 %copy-start.19 = (bf16[197,768]{1,0:T(8,128)(2,1)S(1)}, bf16[197,768]{1,0:T(8,128)(2,1)}, u32[]{:S(2)}) copy-start(bf16[197,768]{1,0:T(8,128)(2,1)} %param.29) | copy-start | bytes 907780
  149.3 89.6 %all-to-all-start = ((bf16[16,64,768]{2,1,0:T(8,128)(2,1)}), bf16[16,64,768]{2,1,0:T(8,128)(2,1)}, u32[]{:S(2)}, u32[]{:S(2)}) async-start(bf16[16,64,768]{2,1,0:T(8,128)(2,1)} %broadcast_select_fusion.1), calls=%async_computation | async-start | bytes 3145728 | tf_op jit(solution)/shard_map/all_to_all | solution.py:61
  153.8 30.9 %collective-permute-start = (bf16[48,16]{0,1:T(8,128)(2,1)S(1)}, bf16[48,16]{0,1:T(8,128)(2,1)S(1)}, u32[]{:S(2)}, u32[]{:S(2)}) collective-permute-start(bf16[48,16]{0,1:T(8,128)(2,1)S(1)} %copy-done.38), channel_id=1, source_target_pairs={{0,2},{2,4},{4,6},{6,8},{8,10},{10,12},{12,14},{14,16},{16,18},{18... | collective-permute-start | bytes 4616 | tf_op jit(solution)/shard_map/ppermute | solution.py:23
  184.8 5.8 collective-permute-start.1
  184.8 5.8 collective-permute-start.8
  190.6 5.7 collective-permute-start.2
  190.6 5.8 collective-permute-start.9
  196.3 5.7 collective-permute-start.3
  196.4 13.3 %collective-permute-start.10 = (bf16[48,16]{0,1:T(8,128)(2,1)S(1)}, bf16[48,16]{0,1:T(8,128)(2,1)S(1)}, u32[]{:S(2)}, u32[]{:S(2)}) collective-permute-start(bf16[48,16]{0,1:T(8,128)(2,1)S(1)} %collective-permute-done.9), channel_id=1, source_target_pairs={{2,0},{4,2},{6,4},{8,6},{10,8},{12,10},{14,12},{16,14},{18,16},{20... | collective-permute-start | bytes 4616 | tf_op jit(solution)/shard_map/ppermute | solution.py:25
  202.1 10.9 %collective-permute-start.4 = (bf16[48,16]{0,1:T(8,128)(2,1)S(1)}, bf16[48,16]{0,1:T(8,128)(2,1)S(1)}, u32[]{:S(2)}, u32[]{:S(2)}) collective-permute-start(bf16[48,16]{0,1:T(8,128)(2,1)S(1)} %collective-permute-done.3), channel_id=1, source_target_pairs={{0,2},{2,4},{4,6},{6,8},{8,10},{10,12},{12,14},{14,16},{16,18},{18... | collective-permute-start | bytes 4616 | tf_op jit(solution)/shard_map/ppermute | solution.py:23
  209.7 4.6 collective-permute-start.11
  213.0 5.7 collective-permute-start.5
  214.3 5.7 collective-permute-start.12
  218.7 5.7 collective-permute-start.6
  220.1 14.3 %collective-permute-start.13 = (bf16[48,16]{0,1:T(8,128)(2,1)S(1)}, bf16[48,16]{0,1:T(8,128)(2,1)S(1)}, u32[]{:S(2)}, u32[]{:S(2)}) collective-permute-start(bf16[48,16]{0,1:T(8,128)(2,1)S(1)} %collective-permute-done.12), channel_id=1, source_target_pairs={{2,0},{4,2},{6,4},{8,6},{10,8},{12,10},{14,12},{16,14},{18,16},{20... | collective-permute-start | bytes 4616 | tf_op jit(solution)/shard_map/ppermute | solution.py:25
  224.5 14.4 %collective-permute-start.7 = (bf16[48,16]{0,1:T(8,128)(2,1)S(1)}, bf16[48,16]{0,1:T(8,128)(2,1)S(1)}, u32[]{:S(2)}, u32[]{:S(2)}) collective-permute-start(bf16[48,16]{0,1:T(8,128)(2,1)S(1)} %collective-permute-done.6), channel_id=1, source_target_pairs={{0,2},{2,4},{4,6},{6,8},{8,10},{10,12},{12,14},{14,16},{16,18},{18... | collective-permute-start | bytes 4616 | tf_op jit(solution)/shard_map/ppermute | solution.py:23
  234.4 18.7 %collective-permute-start.14 = (bf16[48,16]{0,1:T(8,128)(2,1)S(1)}, bf16[48,16]{0,1:T(8,128)(2,1)S(1)}, u32[]{:S(2)}, u32[]{:S(2)}) collective-permute-start(bf16[48,16]{0,1:T(8,128)(2,1)S(1)} %collective-permute-done.13), channel_id=1, source_target_pairs={{2,0},{4,2},{6,4},{8,6},{10,8},{12,10},{14,12},{16,14},{18,16},{20... | collective-permute-start | bytes 4616 | tf_op jit(solution)/shard_map/ppermute | solution.py:25
  248.4 36.5 %all-to-all-start.1 = ((bf16[16,64,768]{2,1,0:T(8,128)(2,1)}), bf16[16,64,768]{2,1,0:T(8,128)(2,1)}, u32[]{:S(2)}, u32[]{:S(2)}) async-start(bf16[16,64,768]{2,1,0:T(8,128)(2,1)} %bitcast.156), calls=%async_computation.1 | async-start | bytes 3145728 | tf_op jit(solution)/shard_map/all_to_all | solution.py:76
  377.1 37.0 %all-to-all-start.3 = ((bf16[16,64,768]{2,1,0:T(8,128)(2,1)}), bf16[16,64,768]{2,1,0:T(8,128)(2,1)S(1)}, u32[]{:S(2)}, u32[]{:S(2)}) async-start(bf16[16,64,768]{2,1,0:T(8,128)(2,1)} %bitcast.157), calls=%async_computation.3 | async-start | bytes 3145728 | tf_op jit(solution)/shard_map/all_to_all | solution.py:76
  382.1 215.1 %reduce-scatter.14.cloned.1.call-start = ((), (), s32[]{:S(2)}) async-start(), calls=%async_computation.8 | async-start | bytes 1253376 | tf_op jit(solution)/shard_map/reduce_scatter | solution.py:256
  447.3 3.9 collective-permute-start.17
  468.1 133.5 %reduce-scatter.12.cloned.1.call-start = ((), (), s32[]{:S(2)}) async-start(), calls=%async_computation.7 | async-start | bytes 3760128 | tf_op jit(solution)/shard_map/reduce_scatter | solution.py:255
  528.7 12.3 %collective-permute-start.18 = (bf16[3,768]{1,0:T(4,128)(2,1)S(1)}, bf16[3,768]{1,0:T(4,128)(2,1)S(1)}, u32[]{:S(2)}, u32[]{:S(2)}) collective-permute-start(bf16[3,768]{1,0:T(4,128)(2,1)S(1)} %slice.39), channel_id=1, source_target_pairs={{0,1},{2,3},{4,5},{6,7},{8,9},{10,11},{12,13},{14,15},{16,17},{18,... | collective-permute-start | bytes 13832
  539.7 54.8 %copy-start.37 = (f32[197]{0:T(256)S(1)}, f32[197]{0:T(256)}, u32[]{:S(2)}) copy-start(f32[197]{0:T(256)} %copy-done.36) | copy-start | bytes 2368
  539.7 50.9 %collective-permute-start.16 = (bf16[3,768]{1,0:T(4,128)(2,1)S(1)}, bf16[3,768]{1,0:T(4,128)(2,1)S(1)}, u32[]{:S(2)}, u32[]{:S(2)}) collective-permute-start(bf16[3,768]{1,0:T(4,128)(2,1)S(1)} %slice.37), channel_id=1, source_target_pairs={{0,1},{2,3},{4,5},{6,7},{8,9},{10,11},{12,13},{14,15},{16,17},{18,... | collective-permute-start | bytes 13832
  541.0 60.6 %copy-start.1 = (bf16[1,1536,768]{2,1,0:T(8,128)(2,1)S(1)}, bf16[1,1536,768]{2,1,0:T(8,128)(2,1)}, u32[]{:S(2)}) copy-start(bf16[1,1536,768]{2,1,0:T(8,128)(2,1)} %param.25) | copy-start | bytes 7077892
  (37 other events, 403.1 us)
Sparse Core Ops, SparseCore 0:
  10.4 43.3 all-gather.5
  468.2 61.6 reduce-scatter.13
  534.3 67.1 reduce-scatter.11
